TPU v7x, 32 devices: a whole 2x2x4 slice. The times are simulated.
32 devices in a mesh: gx: 16 (over z, y, core), gz: 2 (over x).
Axes of the slice: x: 2, y: 2, z: 4, core: 2. Of those that a mesh axis runs over, the one named last changes fastest.
Arguments:
- adjoint: bfloat16 [3, 128, 64, 256], P(None, 'gx', 'gz'), may hold values from -6 to 6
- strain: bfloat16 [128, 64, 256], P('gx', 'gz'), may hold values from -6 to 6
- correction: float32 [64, 256], P('gz'), may hold values from 0.3 to 3
- metric: float32 [256], replicated, may hold values from 0.5 to 4
- stream_inverse: bfloat16 [128, 128], replicated, may hold values from -0.081 to 1.081
- span_inverse: bfloat16 [64, 64], replicated, may hold values from -0.081 to 1.081
- wall_operator: bfloat16 [256, 256], replicated, may hold values from -0.081 to 1.081
Outputs:
- adjoint_next: bfloat16 [3, 128, 64, 256], P(None, 'gx', 'gz')
- gradient: float32 [64, 256], P('gz', 'gx')
All inputs are finite; a program needn't handle non-finite values.
Results may differ from a plain program's by a relative error of at most 0.013.
Values may be sent and summed in bfloat16 or wider, within the bound.
A program may use at most 64 MiB of HBM per device.

v0:
```python
import jax
import jax.numpy as jnp
from jax import lax
from jax.sharding import PartitionSpec as P

near_coef = 7.0 / 9.0
far_coef = 1.0 / 36.0
time_step = 0.25


def stencil(source, axis):
    widened = source.astype(jnp.float32)
    near_diff = jnp.roll(widened, -1, axis) - jnp.roll(widened, 1, axis)
    far_diff = jnp.roll(widened, -2, axis) - jnp.roll(widened, 2, axis)
    return (near_coef * near_diff + far_coef * far_diff).astype(jnp.bfloat16)


def stream_derivative(pencil, stream_inverse):
    right_side = stencil(pencil, 1)
    product = jnp.einsum(
        "ij,kjp->kip", stream_inverse, right_side, preferred_element_type=jnp.float32
    )
    return product.astype(jnp.bfloat16)


def span_derivative(pencil, span_inverse):
    right_side = stencil(pencil, 2)
    product = jnp.einsum(
        "ij,kajy->kaiy", span_inverse, right_side, preferred_element_type=jnp.float32
    )
    return product.astype(jnp.bfloat16)


def wall_derivative(source, wall_operator, metric):
    product = jnp.einsum("kxzj,ij->kxzi", source, wall_operator, preferred_element_type=jnp.float32)
    return product * metric


def span_apply(source, span_inverse):
    derived = span_derivative(
        lax.all_to_all(source, "gz", split_axis=1, concat_axis=2, tiled=True), span_inverse
    )
    return lax.all_to_all(derived, "gz", split_axis=2, concat_axis=1, tiled=True)


def on_device(adjoint, strain, correction, metric, stream_inverse, span_inverse, wall_operator):
    components, stream_cells, span_cells, wall_cells = adjoint.shape
    strain_wide = strain.astype(jnp.float32)
    viscosity = (correction[None] * strain_wide).astype(jnp.bfloat16)
    viscous = viscosity.astype(jnp.float32)[None]
    joined = jnp.concatenate([adjoint, viscosity[None]], 0)
    joined = joined.reshape(components + 1, stream_cells, span_cells * wall_cells)
    pencil = lax.all_to_all(joined, "gx", split_axis=2, concat_axis=1, tiled=True)
    stream_grad = stream_derivative(pencil[:components], stream_inverse)
    pencil_flux = pencil[components:].astype(jnp.float32) * stream_grad.astype(jnp.float32)
    stream_flux = pencil_flux.astype(jnp.bfloat16)
    stream_diverge = stream_derivative(stream_flux, stream_inverse)
    returned = lax.all_to_all(
        jnp.concatenate([stream_grad, stream_diverge], 0),
        "gx",
        split_axis=1,
        concat_axis=2,
        tiled=True,
    )
    returned = returned.reshape(2 * components, stream_cells, span_cells, wall_cells)
    stream_grad = returned[:components]
    stream_diverge = returned[components:]
    span_grad = span_apply(adjoint, span_inverse)
    span_flux = (viscous * span_grad.astype(jnp.float32)).astype(jnp.bfloat16)
    span_diverge = span_apply(span_flux, span_inverse)
    wall_grad = wall_derivative(adjoint, wall_operator, metric).astype(jnp.bfloat16)
    wall_flux = (viscous * wall_grad.astype(jnp.float32)).astype(jnp.bfloat16)
    wall_diverge = wall_derivative(wall_flux, wall_operator, metric)
    total = stream_diverge.astype(jnp.float32) + wall_diverge + span_diverge.astype(jnp.float32)
    updated = (adjoint.astype(jnp.float32) + time_step * total).astype(jnp.bfloat16)
    squares = stream_grad.astype(jnp.float32) ** 2 + wall_grad.astype(jnp.float32) ** 2
    squares = jnp.sum(squares + span_grad.astype(jnp.float32) ** 2, axis=0)
    partial_sum = jnp.sum(strain_wide * squares, axis=0)
    summed = lax.psum_scatter(partial_sum, "gx", scatter_dimension=1, tiled=True)
    gradient = -summed / (stream_cells * lax.axis_size("gx"))
    return (updated, gradient)


def solution(mesh):
    in_specs = (P(None, "gx", "gz", None), P("gx", "gz", None), P("gz", None), P(), P(), P(), P())
    out_specs = (P(None, "gx", "gz", None), P("gz", "gx"))
    return jax.shard_map(
        on_device, mesh=mesh, in_specs=in_specs, out_specs=out_specs, check_vma=False
    )
```

profile of v0, /device:TPU:0, one launch (start us, length us, event | category | flops | bytes accessed | tf_op | source)
XLA Modules:
  0.0 203.0 jit_solution(6696756083981876927)
XLA Ops:
  7.2 0.0 copy-start
  7.2 1.8 copy.55
  9.0 4.2 %all-to-all-start.2 = ((bf16[3,8,32,256]{3,2,0,1:T(8,128)(2,1)}), bf16[3,8,32,256]{3,2,0,1:T(8,128)(2,1)S(1)}, u32[]{:S(2)}, u32[]{:S(2)}) async-start(bf16[3,8,32,256]{3,2,0,1:T(8,128)(2,1)} %copy.55), calls=%async_computation.2 | async-start | bytes 786432 | tf_op jit(solution)/shard_map/all_to_all | solution.py:41
  13.2 1.2 concatenate.67
  14.4 0.9 fusion.55
  15.3 0.1 concatenate.68
  15.4 8.2 %copy.49 = bf16[4,8,8192]{1,0,2:T(4,128)(2,1)} copy(bf16[4,8,8192]{2,1,0:T(8,128)(2,1)S(1)} %pad_maximum_fusion.1) | data formatting | bytes 1048576 | tf_op jit(solution)/shard_map/concatenate | solution.py:51
  23.6 11.2 %reshape.64 = bf16[16,2,8192]{2,1,0:T(2,128)(2,1)} reshape(bf16[8192,4,8]{2,1,0:T(4,128)(2,1)} %bitcast.78) | data formatting | bytes 1048576
  34.8 0.0 all-to-all-done.2
  34.8 6.7 %all-to-all-start = ((bf16[16,2,8192]{2,1,0:T(2,128)(2,1)}), bf16[16,2,8192]{2,1,0:T(2,128)(2,1)S(1)}, u32[]{:S(2)}, u32[]{:S(2)}) async-start(bf16[16,2,8192]{2,1,0:T(2,128)(2,1)} %reshape.64), calls=%async_computation | async-start | bytes 1048576 | tf_op jit(solution)/shard_map/all_to_all | solution.py:53
  41.5 0.1 convert_bitcast_fusion.1
  41.5 0.1 copy.56
  41.6 0.1 fusion.70
  41.8 0.1 fusion.72
  41.9 0.0 copy-done.5
  41.9 0.5 fusion.9
  42.4 1.1 copy.57
  43.5 12.4 %all-to-all-done = bf16[16,2,8192]{2,1,0:T(2,128)(2,1)S(1)} async-done(((bf16[16,2,8192]{2,1,0:T(2,128)(2,1)}), bf16[16,2,8192]{2,1,0:T(2,128)(2,1)S(1)}, u32[]{:S(2)}, u32[]{:S(2)}) %all-to-all-start) | async-done | bytes 524320 | tf_op jit(solution)/shard_map/all_to_all | solution.py:53
  55.9 3.5 %all-to-all-start.3 = ((bf16[3,4,64,256]{3,1,0,2:T(4,128)(2,1)}), bf16[3,4,64,256]{3,1,0,2:T(4,128)(2,1)S(1)}, u32[]{:S(2)}, u32[]{:S(2)}) async-start(bf16[3,4,64,256]{3,1,0,2:T(4,128)(2,1)} %copy.57), calls=%async_computation.3 | async-start | bytes 786432 | tf_op jit(solution)/shard_map/all_to_all | solution.py:43
  59.4 11.0 %reshape.65 = bf16[8192,4,8]{2,1,0:T(4,128)(2,1)} reshape(bf16[16,2,8192]{2,1,0:T(2,128)(2,1)S(1)} %all-to-all-done) | data formatting | bytes 1048576
  70.4 10.7 %copy.50 = bf16[4,8,16,512]{3,1,2,0:T(8,128)(2,1)S(1)} copy(bf16[4,8,16,512]{1,0,3,2:T(4,128)(2,1)} %bitcast.79) | data formatting | bytes 1048576 | tf_op jit(solution)/shard_map/all_to_all | solution.py:53
  81.1 0.1 fusion.28
  81.2 0.2 fusion.62
  81.4 0.2 fusion.64
  81.7 0.0 copy-done.4
  81.7 0.5 fusion.27
  82.2 0.2 fusion.58
  82.4 0.0 copy-start.1
  82.4 0.2 fusion.60
  82.6 0.5 fusion.8
  83.1 0.0 copy-start.3
  83.1 0.1 pad_maximum_fusion
  83.2 1.4 copy.53
  84.6 0.0 all-to-all-done.3
  84.6 4.1 %all-to-all-start.1 = ((bf16[6,128,512]{2,0,1:T(8,128)(2,1)}), bf16[6,128,512]{2,0,1:T(8,128)(2,1)S(1)}, u32[]{:S(2)}, u32[]{:S(2)}) async-start(bf16[6,128,512]{2,0,1:T(8,128)(2,1)} %copy.53), calls=%async_computation.1 | async-start | bytes 2097152 | tf_op jit(solution)/shard_map/all_to_all | solution.py:58
  88.7 0.0 copy-done.2
  88.7 1.1 copy.58
  89.8 21.8 %all-to-all-done.1 = bf16[6,128,512]{2,0,1:T(8,128)(2,1)S(1)} async-done(((bf16[6,128,512]{2,0,1:T(8,128)(2,1)}), bf16[6,128,512]{2,0,1:T(8,128)(2,1)S(1)}, u32[]{:S(2)}, u32[]{:S(2)}) %all-to-all-start.1) | async-done | bytes 786464 | tf_op jit(solution)/shard_map/all_to_all | solution.py:58
  111.6 0.4 copy.71
  112.1 0.1 convert_multiply_fusion
  112.2 1.0 integer_pow.13
  113.2 1.5 add_reduce_fusion
  114.8 0.8 copy.59
  115.5 4.2 %all-to-all-start.4 = ((bf16[3,8,32,256]{3,2,0,1:T(8,128)(2,1)}), bf16[3,8,32,256]{3,2,0,1:T(8,128)(2,1)}, u32[]{:S(2)}, u32[]{:S(2)}) async-start(bf16[3,8,32,256]{3,2,0,1:T(8,128)(2,1)} %copy.59), calls=%async_computation.4 | async-start | bytes 786432 | tf_op jit(solution)/shard_map/all_to_all | solution.py:41
  119.7 0.0 reduce-scatter.4.cloned.1.call-start
  119.8 0.8 copy.68
  120.5 0.0 reduce-scatter.4.cloned.1.call-update
  120.6 0.1 slice_convert_fusion
  120.7 0.0 copy-start.6
  120.7 0.1 reshape.50
  120.8 61.0 %reduce-scatter.4.cloned.1.call-done = f32[16,32]{1,0:T(8,128)} async-done(((f32[256,32]{1,0:T(8,128)}), f32[16,32]{1,0:T(8,128)}) %reduce-scatter.4.cloned.1.call-update) | async-done | bytes 2064
  181.8 0.8 copy.69
  182.5 0.0 all-to-all-done.4
  182.5 1.1 convert_bitcast_fusion
  183.6 0.1 copy.60
  183.7 0.1 fusion.66
  183.8 0.1 fusion.68
  184.0 0.5 fusion.10
  184.5 1.1 copy.61
  185.6 3.5 %all-to-all-start.5 = ((bf16[3,4,64,256]{3,1,0,2:T(4,128)(2,1)}), bf16[3,4,64,256]{3,1,0,2:T(4,128)(2,1)S(1)}, u32[]{:S(2)}, u32[]{:S(2)}) async-start(bf16[3,4,64,256]{3,1,0,2:T(4,128)(2,1)} %copy.61), calls=%async_computation.5 | async-start | bytes 786432 | tf_op jit(solution)/shard_map/all_to_all | solution.py:43
  189.1 0.7 copy.63
  189.7 5.2 %all-to-all-done.5 = bf16[3,4,64,256]{3,1,0,2:T(4,128)(2,1)S(1)} async-done(((bf16[3,4,64,256]{3,1,0,2:T(4,128)(2,1)}), bf16[3,4,64,256]{3,1,0,2:T(4,128)(2,1)S(1)}, u32[]{:S(2)}, u32[]{:S(2)}) %all-to-all-start.5) | async-done | bytes 393248 | tf_op jit(solution)/shard_map/all_to_all | solution.py:43
  194.9 0.1 copy.62
  195.0 1.1 fusion.6
  (19 shorter events, 0.2 us)
Async XLA Ops:
  7.2 106.0 %copy-start = (bf16[256,256]{1,0:T(8,128)(2,1)S(1)}, bf16[256,256]{1,0:T(8,128)(2,1)}, u32[]{:S(2)}) copy-start(bf16[256,256]{1,0:T(8,128)(2,1)} %param.13) | copy-start | bytes 393220
  9.0 25.8 %all-to-all-start.2 = ((bf16[3,8,32,256]{3,2,0,1:T(8,128)(2,1)}), bf16[3,8,32,256]{3,2,0,1:T(8,128)(2,1)S(1)}, u32[]{:S(2)}, u32[]{:S(2)}) async-start(bf16[3,8,32,256]{3,2,0,1:T(8,128)(2,1)} %copy.55), calls=%async_computation.2 | async-start | bytes 786432 | tf_op jit(solution)/shard_map/all_to_all | solution.py:41
  23.6 18.3 %copy-start.5 = (bf16[64,64]{1,0:T(8,128)(2,1)S(1)}, bf16[64,64]{1,0:T(8,128)(2,1)}, u32[]{:S(2)}) copy-start(bf16[64,64]{1,0:T(8,128)(2,1)} %param.12) | copy-start | bytes 24580
  34.8 21.1 %all-to-all-start = ((bf16[16,2,8192]{2,1,0:T(2,128)(2,1)}), bf16[16,2,8192]{2,1,0:T(2,128)(2,1)S(1)}, u32[]{:S(2)}, u32[]{:S(2)}) async-start(bf16[16,2,8192]{2,1,0:T(2,128)(2,1)} %reshape.64), calls=%async_computation | async-start | bytes 1048576 | tf_op jit(solution)/shard_map/all_to_all | solution.py:53
  55.9 28.7 %all-to-all-start.3 = ((bf16[3,4,64,256]{3,1,0,2:T(4,128)(2,1)}), bf16[3,4,64,256]{3,1,0,2:T(4,128)(2,1)S(1)}, u32[]{:S(2)}, u32[]{:S(2)}) async-start(bf16[3,4,64,256]{3,1,0,2:T(4,128)(2,1)} %copy.57), calls=%async_computation.3 | async-start | bytes 786432 | tf_op jit(solution)/shard_map/all_to_all | solution.py:43
  70.4 11.3 %copy-start.4 = (bf16[128,128]{1,0:T(8,128)(2,1)S(1)}, bf16[128,128]{1,0:T(8,128)(2,1)}, u32[]{:S(2)}) copy-start(bf16[128,128]{1,0:T(8,128)(2,1)} %param.11) | copy-start | bytes 98308
  82.4 30.8 %copy-start.1 = (bf16[3,8,32,256]{3,2,1,0:T(8,128)(2,1)S(1)}, bf16[3,8,32,256]{3,2,1,0:T(8,128)(2,1)}, u32[]{:S(2)}) copy-start(bf16[3,8,32,256]{3,2,1,0:T(8,128)(2,1)} %param.7) | copy-start | bytes 1179652
  83.1 36.7 %copy-start.3 = (bf16[8,32,256]{2,1,0:T(8,128)(2,1)S(1)}, bf16[8,32,256]{2,1,0:T(8,128)(2,1)}, u32[]{:S(2)}) copy-start(bf16[8,32,256]{2,1,0:T(8,128)(2,1)} %param.8) | copy-start | bytes 393220
  84.6 4.1 %copy-start.2 = (bf16[3,4,64,256]{3,1,0,2:T(4,128)(2,1)}, bf16[3,4,64,256]{3,1,0,2:T(4,128)(2,1)S(1)}, u32[]{:S(2)}) copy-start(bf16[3,4,64,256]{3,1,0,2:T(4,128)(2,1)S(1)} %all-to-all-done.3) | copy-start | bytes 1179652
  84.6 27.0 %all-to-all-start.1 = ((bf16[6,128,512]{2,0,1:T(8,128)(2,1)}), bf16[6,128,512]{2,0,1:T(8,128)(2,1)S(1)}, u32[]{:S(2)}, u32[]{:S(2)}) async-start(bf16[6,128,512]{2,0,1:T(8,128)(2,1)} %copy.53), calls=%async_computation.1 | async-start | bytes 2097152 | tf_op jit(solution)/shard_map/all_to_all | solution.py:58
  115.5 67.0 %all-to-all-start.4 = ((bf16[3,8,32,256]{3,2,0,1:T(8,128)(2,1)}), bf16[3,8,32,256]{3,2,0,1:T(8,128)(2,1)}, u32[]{:S(2)}, u32[]{:S(2)}) async-start(bf16[3,8,32,256]{3,2,0,1:T(8,128)(2,1)} %copy.59), calls=%async_computation.4 | async-start | bytes 786432 | tf_op jit(solution)/shard_map/all_to_all | solution.py:41
  119.7 62.1 %reduce-scatter.4.cloned.1.call-start = ((), (), s32[]{:S(2)}) async-start(), calls=%async_computation.7 | async-start | bytes 139264
  120.7 74.3 %copy-start.6 = (f32[256]{0:T(256)S(1)}, f32[256]{0:T(256)}, u32[]{:S(2)}) copy-start(f32[256]{0:T(256)} %param.10) | copy-start | bytes 3076
  185.6 9.3 %all-to-all-start.5 = ((bf16[3,4,64,256]{3,1,0,2:T(4,128)(2,1)}), bf16[3,4,64,256]{3,1,0,2:T(4,128)(2,1)S(1)}, u32[]{:S(2)}, u32[]{:S(2)}) async-start(bf16[3,4,64,256]{3,1,0,2:T(4,128)(2,1)} %copy.61), calls=%async_computation.5 | async-start | bytes 786432 | tf_op jit(solution)/shard_map/all_to_all | solution.py:43
Sparse Core Ops, SparseCore 0:
  124.0 57.7 reduce-scatter.3
where the time goes:
time: 204 us; the launch traced here: 203 us
  waiting for transfers between devices  100 us (49%)
  local copies, waits for them, and re-layouts  54.9 us (27%)
  starting transfers between devices  26.1 us (13%)
  between operations  14.4 us (7%)
  matrix products  4.63 us (2%)
  other arithmetic  2.52 us (1%)
    unnamed x2, waiting for transfers between devices  61 us
    unnamed x20, local copies, waits for them, and re-layouts  26.2 us
    all_to_all x1, waiting for transfers between devices, on_device(): lax.all_to_all(jnp.concatenate([stream_grad, stream_diverge], 0), 'gx', s...  21.8 us
    all_to_all x1, waiting for transfers between devices, on_device(): lax.all_to_all(joined, 'gx', split_axis=2, concat_axis=1, tiled=True)  12.4 us
    all_to_all x1, local copies, waits for them, and re-layouts, on_device(): lax.all_to_all(joined, 'gx', split_axis=2, concat_axis=1, tiled=True)  10.7 us
    concatenate x3, local copies, waits for them, and re-layouts, on_device(): joined = jnp.concatenate([adjoint, viscosity[None]], 0)  9.42 us
    all_to_all x2, starting transfers between devices, span_apply(): lax.all_to_all(source, 'gz', split_axis=1, concat_axis=2, tiled=True)  8.36 us
    all_to_all x2, starting transfers between devices, span_apply(): lax.all_to_all(derived, 'gz', split_axis=2, concat_axis=1, tiled=True)  6.93 us
  transfers between devices with their start and end apart: 7, of which 4 were waited for; matrix products, arithmetic and copies ran while one was open for 26% of the time, Pallas kernels for 0%

commit v1 on v0

--- a/solution.py
+++ b/solution.py
@@ -1,6 +1,10 @@
+import functools
+
 import jax
 import jax.numpy as jnp
 from jax import lax
+from jax.experimental import pallas as pl
+from jax.experimental.pallas import tpu as pltpu
 from jax.sharding import PartitionSpec as P
 
 near_coef = 7.0 / 9.0
@@ -81,9 +85,364 @@
     return (updated, gradient)
 
 
+MESH = pl.DeviceIdType.MESH
+F32 = jnp.float32
+BF16 = jnp.bfloat16
+
+
+def positions(rows, columns):
+    return (
+        lax.broadcasted_iota(jnp.int32, (rows, columns), 0),
+        lax.broadcasted_iota(jnp.int32, (rows, columns), 1),
+    )
+
+
+def as_matrix(condition):
+    return jnp.where(condition, 1.0, 0.0).astype(BF16)
+
+
+def matmul(left, right):
+    return jnp.dot(left, right, preferred_element_type=F32)
+
+
+def matmul_transposed(left, right):
+    return lax.dot_general(left, right, (((1,), (1,)), ((), ())), preferred_element_type=F32)
+
+
+def folded(inverse):
+    wide = inverse.astype(F32)
+    order = wide.shape[1]
+    row, column = positions(order, order)
+    gap = lax.rem(row - column + order, order)
+    near = as_matrix(gap == order - 1).astype(F32) - as_matrix(gap == 1).astype(F32)
+    far = as_matrix(gap == order - 2).astype(F32) - as_matrix(gap == 2).astype(F32)
+    both = near_coef * matmul(inverse, near.astype(BF16)) + far_coef * matmul(
+        inverse, far.astype(BF16)
+    )
+    return both.astype(BF16)
+
+
+def kernel(
+    n,
+    adjoint,
+    strain,
+    correction,
+    metric,
+    stream_inverse,
+    span_inverse,
+    wall_operator,
+    updated,
+    gradient,
+    out_x,
+    got_x,
+    back_x,
+    home_x,
+    span,
+    span_matrix,
+    span_held,
+    total,
+    parts_out,
+    parts_in,
+    x_send,
+    x_recv,
+    b_send,
+    b_recv,
+    z_send,
+    z_recv,
+    g_send,
+    g_recv,
+):
+    me = lax.axis_index("gx")
+    side = lax.axis_index("gz")
+    other = 1 - side
+    components, cells, spans, walls = adjoint.shape
+    rows = cells * spans
+    width = spans // n
+    block = cells * width
+    lines = n * block
+
+    barrier = pltpu.get_barrier_semaphore()
+
+    def greet(step, carry):
+        peer = lax.rem(me + step, n)
+        pl.semaphore_signal(barrier, inc=1, device_id=(peer, side), device_id_type=MESH)
+        return carry
+
+    lax.fori_loop(1, n, greet, 0)
+    pl.semaphore_signal(barrier, inc=1, device_id=(me, other), device_id_type=MESH)
+
+    row, column = positions(rows, rows)
+    source_row = (
+        lax.rem(lax.div(row, width), cells) * spans
+        + lax.div(row, block) * width
+        + lax.rem(row, width)
+    )
+    to_blocks = as_matrix(column == source_row)
+    source_column = (
+        lax.rem(lax.div(column, width), cells) * spans
+        + lax.div(column, block) * width
+        + lax.rem(column, width)
+    )
+    from_blocks = as_matrix(row == source_column)
+
+    def blocked(field):
+        return matmul(to_blocks, field).astype(BF16).reshape(n, block, walls)
+
+    strain_here = strain[...]
+    strain_wide = strain_here.astype(F32)
+    viscous = (correction[...][None] * strain_wide).astype(BF16).reshape(rows, walls)
+    out_x[0] = blocked(strain_here.reshape(rows, walls))
+    out_x[1] = blocked(adjoint[0].reshape(rows, walls))
+    span[0, side] = viscous
+    for c in range(components):
+        span[1 + c, side] = adjoint[c].reshape(rows, walls)
+
+    pl.semaphore_wait(barrier, n)
+
+    def fields_of(chunk):
+        return pl.ds(0, 2) if chunk == 0 else pl.ds(chunk + 1, 1)
+
+    def x_copy(chunk, peer, slot):
+        fields = fields_of(chunk)
+        return pltpu.make_async_remote_copy(
+            src_ref=out_x.at[fields, peer],
+            dst_ref=got_x.at[fields, slot],
+            send_sem=x_send.at[chunk, peer],
+            recv_sem=x_recv.at[chunk, slot],
+            device_id=(peer, side),
+            device_id_type=MESH,
+        )
+
+    def b_copy(chunk, peer, slot):
+        return pltpu.make_async_remote_copy(
+            src_ref=back_x.at[chunk, peer],
+            dst_ref=home_x.at[chunk, slot],
+            send_sem=b_send.at[chunk, peer],
+            recv_sem=b_recv.at[chunk, slot],
+            device_id=(peer, side),
+            device_id_type=MESH,
+        )
+
+    def g_copy(chunk, peer, slot):
+        return pltpu.make_async_remote_copy(
+            src_ref=parts_out.at[peer],
+            dst_ref=parts_in.at[slot],
+            send_sem=g_send.at[peer],
+            recv_sem=g_recv.at[slot],
+            device_id=(peer, side),
+            device_id_type=MESH,
+        )
+
+    def z_copy(field, half):
+        return pltpu.make_async_remote_copy(
+            src_ref=span.at[field, half],
+            dst_ref=span.at[field, half],
+            send_sem=z_send.at[field],
+            recv_sem=z_recv.at[field],
+            device_id=(me, other),
+            device_id_type=MESH,
+        )
+
+    def send_all(copy, chunk):
+        def one(step, carry):
+            peer = lax.rem(me + step, n)
+            copy(chunk, peer, me).start()
+            return carry
+
+        lax.fori_loop(n // 2, n, one, 0)
+        lax.fori_loop(1, n // 2, one, 0)
+
+    def receive_all(copy, chunk):
+        def one(step, carry):
+            peer = lax.rem(me + step, n)
+            copy(chunk, peer, peer).wait_recv()
+            return carry
+
+        lax.fori_loop(1, n, one, 0)
+
+    def sent_all(copy, chunk):
+        def one(step, carry):
+            peer = lax.rem(me + step, n)
+            copy(chunk, peer, me).wait_send()
+            return carry
+
+        lax.fori_loop(1, n, one, 0)
+
+    send_all(x_copy, 0)
+    for field in range(components + 1):
+        z_copy(field, side).start()
+    for c in range(1, components):
+        out_x[1 + c] = blocked(adjoint[c].reshape(rows, walls))
+        send_all(x_copy, c)
+    for field in range(components + 1):
+        got_x[field, me] = out_x[field, me]
+
+    wall = wall_operator[...]
+    stretch = metric[...]
+    squares = jnp.zeros((rows, walls), F32)
+    viscous_wide = viscous.astype(F32)
+    for c in range(components):
+        field = adjoint[c].reshape(rows, walls)
+        slope = (matmul_transposed(field, wall) * stretch).astype(BF16)
+        slope_wide = slope.astype(F32)
+        flux = (viscous_wide * slope_wide).astype(BF16)
+        diverge = matmul_transposed(flux, wall) * stretch
+        total[c] = field.astype(F32) + time_step * diverge
+        squares = squares + slope_wide * slope_wide
+    span_held[0] = squares
+
+    row, column = positions(lines, lines // width)
+    spread = as_matrix(lax.div(row, width) == column)
+    row, column = positions(lines, lines)
+    same = lax.rem(row, width) == lax.rem(column, width)
+    stream = matmul_transposed(
+        matmul(spread, folded(stream_inverse[...])).astype(BF16), spread
+    )
+    stream = jnp.where(same, stream, 0.0).astype(BF16)
+
+    row, column = positions(2 * rows, 2 * spans)
+    spread = as_matrix(lax.div(row, rows) * spans + lax.rem(row, spans) == column)
+    row, column = positions(2 * rows, 2 * rows)
+    same = lax.rem(lax.div(row, spans), cells) == lax.rem(lax.div(column, spans), cells)
+    both = matmul_transposed(
+        matmul(spread, folded(span_inverse[...])).astype(BF16), spread
+    )
+    both = jnp.where(same, both, 0.0).astype(BF16)
+    span_matrix[...] = both.reshape(2, rows, 2 * rows)
+
+    line_row = lax.broadcasted_iota(jnp.int32, (lines, walls), 0)
+    owned = jnp.zeros((lines, walls), F32)
+    for w in range(width):
+        values = correction[pl.ds(me * width + w, 1), :]
+        owned = jnp.where(lax.rem(line_row, width) == w, values, owned)
+
+    receive_all(x_copy, 0)
+    line_strain = got_x[0].reshape(lines, walls).astype(F32)
+    line_viscous = (owned * line_strain).astype(BF16).astype(F32)
+    line_squares = jnp.zeros((lines, walls), F32)
+    for c in range(components):
+        if c > 0:
+            receive_all(x_copy, c)
+        slope = matmul(stream, got_x[1 + c].reshape(lines, walls)).astype(BF16)
+        slope_wide = slope.astype(F32)
+        flux = (line_viscous * slope_wide).astype(BF16)
+        back_x[c] = matmul(stream, flux).astype(BF16).reshape(n, block, walls)
+        send_all(b_copy, c)
+        home_x[c, me] = back_x[c, me]
+        line_squares = line_squares + slope_wide * slope_wide
+    weighted = line_strain * line_squares
+
+    z_copy(0, other).wait_recv()
+    viscous_both = span[0].reshape(2 * rows, walls).astype(F32)
+    for c in range(components):
+        z_copy(1 + c, other).wait_recv()
+        slope = matmul(both, span[1 + c].reshape(2 * rows, walls)).astype(BF16)
+        slope_wide = slope.astype(F32)
+        flux = (viscous_both * slope_wide).astype(BF16)
+        diverge = matmul(span_matrix[side], flux).astype(BF16).astype(F32)
+        total[c] = total[c] + time_step * diverge
+        own = jnp.where(side == 0, slope_wide[:rows], slope_wide[rows:])
+        span_held[0] = span_held[0] + own * own
+
+    partial = jnp.sum(strain_wide * span_held[0].reshape(cells, spans, walls), axis=0)
+    span_row = lax.broadcasted_iota(jnp.int32, (spans, walls), 0)
+    for w in range(width):
+        chosen = jnp.where(lax.rem(line_row, width) == w, weighted, 0.0)
+        summed = jnp.sum(chosen, axis=0, keepdims=True)
+        partial = partial + jnp.where(span_row == me * width + w, summed, 0.0)
+    padded = jnp.concatenate([partial, jnp.zeros((128 - spans, walls), F32)], axis=0)
+    parts_out[...] = padded.T.reshape(n, walls // n, 128)
+    send_all(g_copy, 0)
+    parts_in[me] = parts_out[me]
+
+    for c in range(components):
+        receive_all(b_copy, c)
+        moved = matmul(from_blocks, home_x[c].reshape(lines, walls))
+        result = total[c] + time_step * moved
+        updated[c] = result.astype(BF16).reshape(cells, spans, walls)
+
+    receive_all(g_copy, 0)
+    whole = jnp.sum(parts_in[...], axis=0) * (-1.0 / (cells * n))
+    tall = jnp.concatenate([whole, jnp.zeros((128 - walls // n, 128), F32)], axis=0)
+    gradient[...] = tall.T[:spans, : walls // n]
+
+    for c in range(components):
+        sent_all(x_copy, c)
+        sent_all(b_copy, c)
+    sent_all(g_copy, 0)
+    for field in range(components + 1):
+        z_copy(field, side).wait_send()
+
+
+def in_one_kernel(
+    n, adjoint, strain, correction, metric, stream_inverse, span_inverse, wall_operator
+):
+    components, cells, spans, walls = adjoint.shape
+    rows = cells * spans
+    block = rows // n
+    vmem = pl.BlockSpec(memory_space=pltpu.VMEM)
+    blocks = (n, block, walls)
+    dma = pltpu.SemaphoreType.DMA
+    return tuple(
+        pl.pallas_call(
+            functools.partial(kernel, n),
+            out_shape=(
+                jax.ShapeDtypeStruct(adjoint.shape, BF16),
+                jax.ShapeDtypeStruct((spans, walls // n), F32),
+            ),
+            in_specs=[vmem] * 7,
+            out_specs=(vmem, vmem),
+            scratch_shapes=[
+                pltpu.VMEM((components + 1,) + blocks, BF16),
+                pltpu.VMEM((components + 1,) + blocks, BF16),
+                pltpu.VMEM((components,) + blocks, BF16),
+                pltpu.VMEM((components,) + blocks, BF16),
+                pltpu.VMEM((components + 1, 2, rows, walls), BF16),
+                pltpu.VMEM((2, rows, 2 * rows), BF16),
+                pltpu.VMEM((1, rows, walls), F32),
+                pltpu.VMEM((components, rows, walls), F32),
+                pltpu.VMEM((n, walls // n, 128), F32),
+                pltpu.VMEM((n, walls // n, 128), F32),
+                dma((components, n)),
+                dma((components, n)),
+                dma((components, n)),
+                dma((components, n)),
+                dma((components + 1,)),
+                dma((components + 1,)),
+                dma((n,)),
+                dma((n,)),
+            ],
+            compiler_params=pltpu.CompilerParams(
+                collective_id=0, has_side_effects=True, vmem_limit_bytes=40 * 1024 * 1024
+            ),
+        )(
+            adjoint,
+            strain,
+            correction,
+            metric.reshape(1, walls),
+            stream_inverse,
+            span_inverse,
+            wall_operator,
+        )
+    )
+
+
+def on_each(mesh, adjoint, strain, *rest):
+    n = mesh.shape["gx"]
+    _, cells, spans, walls = adjoint.shape
+    small = mesh.shape["gz"] == 2 and spans % n == 0 and spans <= 128
+    if small and cells * spans // n % 16 == 0 and walls // n % 8 == 0 and walls // n <= 128:
+        return in_one_kernel(n, adjoint, strain, *rest)
+    return on_device(adjoint, strain, *rest)
+
+
 def solution(mesh):
     in_specs = (P(None, "gx", "gz", None), P("gx", "gz", None), P("gz", None), P(), P(), P(), P())
     out_specs = (P(None, "gx", "gz", None), P("gz", "gx"))
     return jax.shard_map(
-        on_device, mesh=mesh, in_specs=in_specs, out_specs=out_specs, check_vma=False
-    )
+        functools.partial(on_each, mesh),
+        mesh=mesh,
+        in_specs=in_specs,
+        out_specs=out_specs,
+        check_vma=False,
+    )

time: 204 us -> 41.3 us (0.20)
  waiting for transfers between devices: 100 us -> 0 us
  local copies, waits for them, and re-layouts: 54.9 us -> 7.12 us
  Pallas kernels: 0 us -> 33.1 us
  starting transfers between devices: 26.1 us -> 0 us
  between operations: 14.4 us -> 0.66 us
  matrix products: 4.63 us -> 0 us
  other arithmetic: 2.52 us -> 0 us
    unnamed x2 -> x0, waiting for transfers between devices: 61 us -> none
    all_to_all x6 -> x0, waiting for transfers between devices: 39.4 us -> none  [the longest x1 21.8 us: on_device(): lax.all_to_all(jnp.concatenate([stream_grad, stream_diverge], 0), 'gx', s...]
    pallas_call x0 -> x1, Pallas kernels: none -> 33.1 us  [in_one_kernel(): pl.pallas_call(functools.partial(kernel, n), out_shape=(jax.ShapeDtypeStr...]
    all_to_all x6 -> x0, starting transfers between devices: 26 us -> none  [the longest x2 8.36 us: span_apply(): lax.all_to_all(source, 'gz', split_axis=1, concat_axis=2, tiled=True)]
    unnamed x20 -> x15, local copies, waits for them, and re-layouts: 26.2 us -> 6.45 us
    all_to_all x2 -> x0, local copies, waits for them, and re-layouts: 11.2 us -> none  [the longest x1 10.7 us: on_device(): lax.all_to_all(joined, 'gx', split_axis=2, concat_axis=1, tiled=True)]
    concatenate x4 -> x0, local copies, waits for them, and re-layouts: 10.8 us -> none  [the longest x3 9.42 us: on_device(): joined = jnp.concatenate([adjoint, viscosity[None]], 0)]
    dot_general x6 -> x0, matrix products: 4.63 us -> none  [the longest x2 2.66 us: wall_derivative(): jnp.einsum('kxzj,ij->kxzi', source, wall_operator, preferred_element_type...]
  transfers between devices with their start and end apart: 7 -> 0, of which waited for: 4 -> 0; matrix products, arithmetic and copies ran while one was open for 26% -> 0% of each run, Pallas kernels for 0% -> 0%
where the time goes in v1:
time: 41.3 us; the launch traced here: 40.9 us
  Pallas kernels  33.1 us (80%)
  local copies, waits for them, and re-layouts  7.12 us (17%)
  between operations  0.66 us (2%)
    pallas_call x1, Pallas kernels, in_one_kernel(): pl.pallas_call(functools.partial(kernel, n), out_shape=(jax.ShapeDtypeStr...  33.1 us
    unnamed x15, local copies, waits for them, and re-layouts  6.45 us

profile of v1, /device:TPU:0, one launch (start us, length us, event | category | flops | bytes accessed | tf_op | source)
XLA Modules:
  0.0 40.9 jit_solution(7045241894165390283)
XLA Ops:
  0.6 0.0 copy-start.6
  0.6 0.7 %copy-done.6 = f32[256]{0:T(256)S(1)} copy-done((f32[256]{0:T(256)S(1)}, f32[256]{0:T(256)}, u32[]{:S(2)}) %copy-start.6) | copy-done | bytes 1048
  1.3 0.0 copy-start
  1.3 1.0 %copy-done = bf16[3,8,32,256]{3,2,1,0:T(8,128)(2,1)S(1)} copy-done((bf16[3,8,32,256]{3,2,1,0:T(8,128)(2,1)S(1)}, bf16[3,8,32,256]{3,2,1,0:T(8,128)(2,1)}, u32[]{:S(2)}) %copy-start) | copy-done | bytes 393240
  2.3 0.0 copy-start.1
  2.3 0.9 %copy-done.1 = bf16[8,32,256]{2,1,0:T(8,128)(2,1)S(1)} copy-done((bf16[8,32,256]{2,1,0:T(8,128)(2,1)S(1)}, bf16[8,32,256]{2,1,0:T(8,128)(2,1)}, u32[]{:S(2)}) %copy-start.1) | copy-done | bytes 131096
  3.2 0.0 copy-start.2
  3.2 0.9 %copy-done.2 = bf16[256,256]{1,0:T(8,128)(2,1)S(1)} copy-done((bf16[256,256]{1,0:T(8,128)(2,1)S(1)}, bf16[256,256]{1,0:T(8,128)(2,1)}, u32[]{:S(2)}) %copy-start.2) | copy-done | bytes 131096
  4.1 0.0 copy-start.3
  4.1 0.8 %copy-done.3 = f32[32,256]{1,0:T(8,128)S(1)} copy-done((f32[32,256]{1,0:T(8,128)S(1)}, f32[32,256]{1,0:T(8,128)}, u32[]{:S(2)}) %copy-start.3) | copy-done | bytes 32792
  4.9 0.0 copy-start.4
  4.9 0.8 %copy-done.4 = bf16[128,128]{1,0:T(8,128)(2,1)S(1)} copy-done((bf16[128,128]{1,0:T(8,128)(2,1)S(1)}, bf16[128,128]{1,0:T(8,128)(2,1)}, u32[]{:S(2)}) %copy-start.4) | copy-done | bytes 32792
  5.6 0.0 copy-start.5
  5.6 0.7 %copy-done.5 = bf16[64,64]{1,0:T(8,128)(2,1)S(1)} copy-done((bf16[64,64]{1,0:T(8,128)(2,1)S(1)}, bf16[64,64]{1,0:T(8,128)(2,1)}, u32[]{:S(2)}) %copy-start.5) | copy-done | bytes 8216
  6.4 33.1 %shard_map.86 = (bf16[3,8,32,256]{3,2,1,0:T(8,128)(2,1)S(1)}, f32[32,16]{1,0:T(8,128)S(1)}) custom-call(bf16[3,8,32,256]{3,2,1,0:T(8,128)(2,1)S(1)} %copy-done, bf16[8,32,256]{2,1,0:T(8,128)(2,1)S(1)} %copy-done.1, f32[32,256]{1,0:T(8,128)S(1)} %copy-done.3, f32[1,256]{1,0:T(1,128)S(1)} %bitcast.1, bf16[128,128]{1,0:T(8,128)(2,1)S(1)} %copy-done.4, ...), custom_call_target="tpu_custom_call" | custom-call | tf_op jit(solution)/shard_map/pallas_call | solution.py:387
  39.5 0.7 %copy.9 = f32[32,16]{0,1:T(8,128)} copy(f32[32,16]{1,0:T(8,128)S(1)} %get-tuple-element.3) | data formatting | bytes 4096 | tf_op jit(solution)/shard_map/pallas_call | solution.py:387
  40.2 0.7 %copy.11 = bf16[3,8,32,256]{3,2,1,0:T(8,128)(2,1)} copy(bf16[3,8,32,256]{3,2,1,0:T(8,128)(2,1)S(1)} %get-tuple-element.6) | data formatting | bytes 786432
Async XLA Ops:
  0.6 0.7 %copy-start.6 = (f32[256]{0:T(256)S(1)}, f32[256]{0:T(256)}, u32[]{:S(2)}) copy-start(f32[256]{0:T(256)} %param.10) | copy-start | bytes 3076
  1.3 1.0 %copy-start = (bf16[3,8,32,256]{3,2,1,0:T(8,128)(2,1)S(1)}, bf16[3,8,32,256]{3,2,1,0:T(8,128)(2,1)}, u32[]{:S(2)}) copy-start(bf16[3,8,32,256]{3,2,1,0:T(8,128)(2,1)} %adjoint.1) | copy-start | bytes 1179652
  2.3 0.9 %copy-start.1 = (bf16[8,32,256]{2,1,0:T(8,128)(2,1)S(1)}, bf16[8,32,256]{2,1,0:T(8,128)(2,1)}, u32[]{:S(2)}) copy-start(bf16[8,32,256]{2,1,0:T(8,128)(2,1)} %strain.1) | copy-start | bytes 393220
  3.2 0.9 %copy-start.2 = (bf16[256,256]{1,0:T(8,128)(2,1)S(1)}, bf16[256,256]{1,0:T(8,128)(2,1)}, u32[]{:S(2)}) copy-start(bf16[256,256]{1,0:T(8,128)(2,1)} %wall_operator.1) | copy-start | bytes 393220
  4.1 0.8 %copy-start.3 = (f32[32,256]{1,0:T(8,128)S(1)}, f32[32,256]{1,0:T(8,128)}, u32[]{:S(2)}) copy-start(f32[32,256]{1,0:T(8,128)} %correction.1) | copy-start | bytes 98308
  4.9 0.8 %copy-start.4 = (bf16[128,128]{1,0:T(8,128)(2,1)S(1)}, bf16[128,128]{1,0:T(8,128)(2,1)}, u32[]{:S(2)}) copy-start(bf16[128,128]{1,0:T(8,128)(2,1)} %stream_inverse.1) | copy-start | bytes 98308
  5.6 0.7 %copy-start.5 = (bf16[64,64]{1,0:T(8,128)(2,1)S(1)}, bf16[64,64]{1,0:T(8,128)(2,1)}, u32[]{:S(2)}) copy-start(bf16[64,64]{1,0:T(8,128)(2,1)} %span_inverse.1) | copy-start | bytes 24580

commit v2 on v1

--- a/solution.py
+++ b/solution.py
@@ -86,6 +86,8 @@
 
 
 MESH = pl.DeviceIdType.MESH
+field_chunks = ((0, 2), (2, 1), (3, 1))
+back_chunks = ((0, 1), (1, 1), (2, 1))
 F32 = jnp.float32
 BF16 = jnp.bfloat16
 
@@ -124,15 +126,26 @@
 
 def kernel(
     n,
+    cells,
     adjoint,
+    strain_far,
+    correction_far,
+    metric_far,
+    stream_far,
+    span_far,
+    wall_far,
+    updated_far,
+    gradient_far,
+    updated,
+    gradient,
+    stored,
     strain,
     correction,
     metric,
     stream_inverse,
     span_inverse,
     wall_operator,
-    updated,
-    gradient,
+    loaded,
     out_x,
     got_x,
     back_x,
@@ -143,6 +156,8 @@
     total,
     parts_out,
     parts_in,
+    tall,
+    short,
     x_send,
     x_recv,
     b_send,
@@ -155,8 +170,8 @@
     me = lax.axis_index("gx")
     side = lax.axis_index("gz")
     other = 1 - side
-    components, cells, spans, walls = adjoint.shape
-    rows = cells * spans
+    components, rows, walls = adjoint.shape
+    spans = rows // cells
     width = spans // n
     block = cells * width
     lines = n * block
@@ -170,6 +185,17 @@
 
     lax.fori_loop(1, n, greet, 0)
     pl.semaphore_signal(barrier, inc=1, device_id=(me, other), device_id_type=MESH)
+
+    loads = [(strain_far, strain), (adjoint.at[0], span.at[1, side]), (correction_far, correction)]
+    loads += [(adjoint.at[c], span.at[1 + c, side]) for c in range(1, components)]
+    loads += [(wall_far, wall_operator), (metric_far, metric)]
+    loads += [(stream_far, stream_inverse), (span_far, span_inverse)]
+    loads = [
+        pltpu.make_async_copy(source, target, loaded.at[k])
+        for k, (source, target) in enumerate(loads)
+    ]
+    for load in loads:
+        load.start()
 
     row, column = positions(rows, rows)
     source_row = (
@@ -188,25 +214,23 @@
     def blocked(field):
         return matmul(to_blocks, field).astype(BF16).reshape(n, block, walls)
 
-    strain_here = strain[...]
-    strain_wide = strain_here.astype(F32)
+    for load in loads[:2]:
+        load.wait()
+    out_x[:, 0] = blocked(strain[...])
+    out_x[:, 1] = blocked(span[1, side])
+    for load in loads[2:]:
+        load.wait()
+    strain_wide = strain[...].astype(F32).reshape(cells, spans, walls)
     viscous = (correction[...][None] * strain_wide).astype(BF16).reshape(rows, walls)
-    out_x[0] = blocked(strain_here.reshape(rows, walls))
-    out_x[1] = blocked(adjoint[0].reshape(rows, walls))
     span[0, side] = viscous
-    for c in range(components):
-        span[1 + c, side] = adjoint[c].reshape(rows, walls)
 
     pl.semaphore_wait(barrier, n)
 
-    def fields_of(chunk):
-        return pl.ds(0, 2) if chunk == 0 else pl.ds(chunk + 1, 1)
-
     def x_copy(chunk, peer, slot):
-        fields = fields_of(chunk)
+        fields = pl.ds(*field_chunks[chunk])
         return pltpu.make_async_remote_copy(
-            src_ref=out_x.at[fields, peer],
-            dst_ref=got_x.at[fields, slot],
+            src_ref=out_x.at[peer, fields],
+            dst_ref=got_x.at[slot, fields],
             send_sem=x_send.at[chunk, peer],
             recv_sem=x_recv.at[chunk, slot],
             device_id=(peer, side),
@@ -214,9 +238,10 @@
         )
 
     def b_copy(chunk, peer, slot):
+        fields = pl.ds(*back_chunks[chunk])
         return pltpu.make_async_remote_copy(
-            src_ref=back_x.at[chunk, peer],
-            dst_ref=home_x.at[chunk, slot],
+            src_ref=back_x.at[peer, fields],
+            dst_ref=home_x.at[slot, fields],
             send_sem=b_send.at[chunk, peer],
             recv_sem=b_recv.at[chunk, slot],
             device_id=(peer, side),
@@ -271,18 +296,18 @@
     send_all(x_copy, 0)
     for field in range(components + 1):
         z_copy(field, side).start()
-    for c in range(1, components):
-        out_x[1 + c] = blocked(adjoint[c].reshape(rows, walls))
-        send_all(x_copy, c)
-    for field in range(components + 1):
-        got_x[field, me] = out_x[field, me]
+    for chunk, (start, count) in enumerate(field_chunks[1:], 1):
+        for field in range(start, start + count):
+            out_x[:, field] = blocked(span[field, side])
+        send_all(x_copy, chunk)
+    got_x[me] = out_x[me]
 
     wall = wall_operator[...]
     stretch = metric[...]
     squares = jnp.zeros((rows, walls), F32)
     viscous_wide = viscous.astype(F32)
     for c in range(components):
-        field = adjoint[c].reshape(rows, walls)
+        field = span[1 + c, side]
         slope = (matmul_transposed(field, wall) * stretch).astype(BF16)
         slope_wide = slope.astype(F32)
         flux = (viscous_wide * slope_wide).astype(BF16)
@@ -316,20 +341,20 @@
         values = correction[pl.ds(me * width + w, 1), :]
         owned = jnp.where(lax.rem(line_row, width) == w, values, owned)
 
-    receive_all(x_copy, 0)
-    line_strain = got_x[0].reshape(lines, walls).astype(F32)
-    line_viscous = (owned * line_strain).astype(BF16).astype(F32)
     line_squares = jnp.zeros((lines, walls), F32)
-    for c in range(components):
-        if c > 0:
-            receive_all(x_copy, c)
-        slope = matmul(stream, got_x[1 + c].reshape(lines, walls)).astype(BF16)
-        slope_wide = slope.astype(F32)
-        flux = (line_viscous * slope_wide).astype(BF16)
-        back_x[c] = matmul(stream, flux).astype(BF16).reshape(n, block, walls)
-        send_all(b_copy, c)
-        home_x[c, me] = back_x[c, me]
-        line_squares = line_squares + slope_wide * slope_wide
+    for chunk, (start, count) in enumerate(back_chunks):
+        receive_all(x_copy, chunk)
+        if chunk == 0:
+            line_strain = got_x[:, 0].reshape(lines, walls).astype(F32)
+            line_viscous = (owned * line_strain).astype(BF16).astype(F32)
+        for c in range(start, start + count):
+            slope = matmul(stream, got_x[:, 1 + c].reshape(lines, walls)).astype(BF16)
+            slope_wide = slope.astype(F32)
+            flux = (line_viscous * slope_wide).astype(BF16)
+            back_x[:, c] = matmul(stream, flux).astype(BF16).reshape(n, block, walls)
+            line_squares = line_squares + slope_wide * slope_wide
+        send_all(b_copy, chunk)
+    home_x[me] = back_x[me]
     weighted = line_strain * line_squares
 
     z_copy(0, other).wait_recv()
@@ -351,27 +376,47 @@
         summed = jnp.sum(chosen, axis=0, keepdims=True)
         partial = partial + jnp.where(span_row == me * width + w, summed, 0.0)
     padded = jnp.concatenate([partial, jnp.zeros((128 - spans, walls), F32)], axis=0)
-    parts_out[...] = padded.T.reshape(n, walls // n, 128)
+    tall[...] = padded.T
+    pack = 128 // spans
+    deep = walls // (n * pack)
+    packed = tall[pl.ds(0, n * deep, stride=pack), :]
+    for w in range(1, pack):
+        piece = tall[pl.ds(w, n * deep, stride=pack), :]
+        packed = packed + pltpu.roll(piece, w * spans, 1)
+    for peer in range(n):
+        parts_out[peer] = packed[peer * deep : (peer + 1) * deep]
     send_all(g_copy, 0)
     parts_in[me] = parts_out[me]
 
-    for c in range(components):
-        receive_all(b_copy, c)
-        moved = matmul(from_blocks, home_x[c].reshape(lines, walls))
-        result = total[c] + time_step * moved
-        updated[c] = result.astype(BF16).reshape(cells, spans, walls)
+    stores = [
+        pltpu.make_async_copy(updated.at[c], updated_far.at[c], stored.at[c])
+        for c in range(components)
+    ]
+    stores.append(pltpu.make_async_copy(gradient, gradient_far, stored.at[components]))
+    for chunk, (start, count) in enumerate(back_chunks):
+        receive_all(b_copy, chunk)
+        for c in range(start, start + count):
+            moved = matmul(from_blocks, home_x[:, c].reshape(lines, walls))
+            result = total[c] + time_step * moved
+            updated[c] = result.astype(BF16)
+            stores[c].start()
 
     receive_all(g_copy, 0)
     whole = jnp.sum(parts_in[...], axis=0) * (-1.0 / (cells * n))
-    tall = jnp.concatenate([whole, jnp.zeros((128 - walls // n, 128), F32)], axis=0)
-    gradient[...] = tall.T[:spans, : walls // n]
-
-    for c in range(components):
-        sent_all(x_copy, c)
-        sent_all(b_copy, c)
+    for w in range(pack):
+        piece = whole if w == 0 else pltpu.roll(whole, 128 - w * spans, 1)
+        short[pl.ds(w, deep, stride=pack), :] = piece
+    gradient[...] = short[:, :spans]
+    stores[components].start()
+
+    for chunk in range(len(back_chunks)):
+        sent_all(x_copy, chunk)
+        sent_all(b_copy, chunk)
     sent_all(g_copy, 0)
     for field in range(components + 1):
         z_copy(field, side).wait_send()
+    for store in stores:
+        store.wait()
 
 
 def in_one_kernel(
@@ -379,58 +424,71 @@
 ):
     components, cells, spans, walls = adjoint.shape
     rows = cells * spans
-    block = rows // n
     vmem = pl.BlockSpec(memory_space=pltpu.VMEM)
-    blocks = (n, block, walls)
+    far = pl.BlockSpec(memory_space=pltpu.HBM)
+    block = (rows // n, walls)
+    deep = walls // n * spans // 128
     dma = pltpu.SemaphoreType.DMA
-    return tuple(
-        pl.pallas_call(
-            functools.partial(kernel, n),
-            out_shape=(
-                jax.ShapeDtypeStruct(adjoint.shape, BF16),
-                jax.ShapeDtypeStruct((spans, walls // n), F32),
-            ),
-            in_specs=[vmem] * 7,
-            out_specs=(vmem, vmem),
-            scratch_shapes=[
-                pltpu.VMEM((components + 1,) + blocks, BF16),
-                pltpu.VMEM((components + 1,) + blocks, BF16),
-                pltpu.VMEM((components,) + blocks, BF16),
-                pltpu.VMEM((components,) + blocks, BF16),
-                pltpu.VMEM((components + 1, 2, rows, walls), BF16),
-                pltpu.VMEM((2, rows, 2 * rows), BF16),
-                pltpu.VMEM((1, rows, walls), F32),
-                pltpu.VMEM((components, rows, walls), F32),
-                pltpu.VMEM((n, walls // n, 128), F32),
-                pltpu.VMEM((n, walls // n, 128), F32),
-                dma((components, n)),
-                dma((components, n)),
-                dma((components, n)),
-                dma((components, n)),
-                dma((components + 1,)),
-                dma((components + 1,)),
-                dma((n,)),
-                dma((n,)),
-            ],
-            compiler_params=pltpu.CompilerParams(
-                collective_id=0, has_side_effects=True, vmem_limit_bytes=40 * 1024 * 1024
-            ),
-        )(
-            adjoint,
-            strain,
-            correction,
-            metric.reshape(1, walls),
-            stream_inverse,
-            span_inverse,
-            wall_operator,
-        )
-    )
+    updated, gradient = pl.pallas_call(
+        functools.partial(kernel, n, cells),
+        out_shape=(
+            jax.ShapeDtypeStruct((components, rows, walls), BF16),
+            jax.ShapeDtypeStruct((walls // n, spans), F32),
+        ),
+        in_specs=[far] * 7,
+        out_specs=(far, far),
+        scratch_shapes=[
+            pltpu.VMEM((components, rows, walls), BF16),
+            pltpu.VMEM((walls // n, spans), F32),
+            dma((components + 1,)),
+            pltpu.VMEM((rows, walls), BF16),
+            pltpu.VMEM(correction.shape, F32),
+            pltpu.VMEM((1, walls), F32),
+            pltpu.VMEM(stream_inverse.shape, BF16),
+            pltpu.VMEM(span_inverse.shape, BF16),
+            pltpu.VMEM(wall_operator.shape, BF16),
+            dma((components + 6,)),
+            pltpu.VMEM((n, components + 1) + block, BF16),
+            pltpu.VMEM((n, components + 1) + block, BF16),
+            pltpu.VMEM((n, components) + block, BF16),
+            pltpu.VMEM((n, components) + block, BF16),
+            pltpu.VMEM((components + 1, 2, rows, walls), BF16),
+            pltpu.VMEM((2, rows, 2 * rows), BF16),
+            pltpu.VMEM((1, rows, walls), F32),
+            pltpu.VMEM((components, rows, walls), F32),
+            pltpu.VMEM((n, deep, 128), F32),
+            pltpu.VMEM((n, deep, 128), F32),
+            pltpu.VMEM((walls, 128), F32),
+            pltpu.VMEM((walls // n, 128), F32),
+            dma((components, n)),
+            dma((components, n)),
+            dma((components, n)),
+            dma((components, n)),
+            dma((components + 1,)),
+            dma((components + 1,)),
+            dma((n,)),
+            dma((n,)),
+        ],
+        compiler_params=pltpu.CompilerParams(
+            collective_id=0, has_side_effects=True, vmem_limit_bytes=64 * 1024 * 1024 - 65536
+        ),
+    )(
+        adjoint.reshape(components, rows, walls),
+        strain.reshape(rows, walls),
+        correction,
+        metric.reshape(1, walls),
+        stream_inverse,
+        span_inverse,
+        wall_operator,
+    )
+    return updated.reshape(adjoint.shape), gradient.T
 
 
 def on_each(mesh, adjoint, strain, *rest):
     n = mesh.shape["gx"]
     _, cells, spans, walls = adjoint.shape
-    small = mesh.shape["gz"] == 2 and spans % n == 0 and spans <= 128
+    small = len(adjoint) == 3 and walls // n * spans % 128 == 0 and 128 % spans == 0 and walls // n * spans >= 128
+    small = small and mesh.shape["gz"] == 2 and spans % n == 0 and spans <= 128
     if small and cells * spans // n % 16 == 0 and walls // n % 8 == 0 and walls // n <= 128:
         return in_one_kernel(n, adjoint, strain, *rest)
     return on_device(adjoint, strain, *rest)

time: 41.3 us -> 34.7 us (0.84)
  local copies, waits for them, and re-layouts: 7.12 us -> 2.37 us
  Pallas kernels: 33.1 us -> 31.5 us
    unnamed x15 -> x4, local copies, waits for them, and re-layouts: 6.45 us -> 2.37 us
    pallas_call x1, Pallas kernels: 33.1 us -> 31.5 us  [in_one_kernel(): pl.pallas_call(functools.partial(kernel, n, cells), out_shape=(jax.ShapeD...]
    pallas_call x1 -> x0, local copies, waits for them, and re-layouts: 0.67 us -> none  [in_one_kernel(): pl.pallas_call(functools.partial(kernel, n), out_shape=(jax.ShapeDtypeStr...]
where the time goes in v2:
time: 34.7 us; the launch traced here: 34.5 us
  Pallas kernels  31.5 us (91%)
  local copies, waits for them, and re-layouts  2.37 us (7%)
  between operations  0.65 us (2%)
    pallas_call x1, Pallas kernels, in_one_kernel(): pl.pallas_call(functools.partial(kernel, n, cells), out_shape=(jax.ShapeD...  31.5 us
    unnamed x4, local copies, waits for them, and re-layouts  2.37 us

profile of v2, /device:TPU:0, one launch (start us, length us, event | category | flops | bytes accessed | tf_op | source)
XLA Modules:
  0.0 34.5 jit_solution(7972834266212202963)
XLA Ops:
  0.6 31.5 %shard_map.86 = (bf16[3,256,256]{2,1,0:T(8,128)(2,1)}, f32[16,32]{1,0:T(8,128)}) custom-call(bf16[3,256,256]{2,1,0:T(8,128)(2,1)} %bitcast.5, bf16[256,256]{1,0:T(8,128)(2,1)} %bitcast.7, f32[32,256]{1,0:T(8,128)} %correction_far.1, f32[1,256]{1,0:T(1,128)} %bitcast.9, bf16[128,128]{1,0:T(8,128)(2,1)} %stream_far.1, bf16[64,64]{1,0:T(8,128)(2,1)} %span_far.1, ...), custom_call_target="tpu_custom_call" | custom-call | tf_op jit(solution)/shard_map/pallas_call | solution.py:432
  32.1 0.0 copy-start
  32.1 1.8 %copy.11 = bf16[3,8,32,256]{3,2,1,0:T(8,128)(2,1)} copy(bf16[3,8,32,256]{3,2,1,0:T(8,128)(2,1)} %bitcast.6) | data formatting | bytes 786432
  33.9 0.0 copy-done
  33.9 0.6 %copy.12 = f32[32,16]{0,1:T(8,128)} copy(f32[32,16]{0,1:T(8,128)S(1)} %bitcast.8) | data formatting | bytes 4096
Async XLA Ops:
  32.1 1.8 %copy-start = (f32[16,32]{1,0:T(8,128)S(1)}, f32[16,32]{1,0:T(8,128)}, u32[]{:S(2)}) copy-start(f32[16,32]{1,0:T(8,128)} %get-tuple-element.5) | copy-start | bytes 6148
